TPU v7x, 512 devices: a whole 4x4x16 slice. The times are simulated.
512 devices in a mesh: memory: 16 (over z), group: 32 (over y, x, core).
Axes of the slice: x: 4, y: 4, z: 16, core: 2. Of those that a mesh axis runs over, the one named last changes fastest.
Arguments:
- queries: bfloat16 [32, 128, 32, 128], P('group', 'memory')
- positives: bfloat16 [32, 128, 128, 128], P('group', 'memory'), may hold values from -6 to 6
- memory: bfloat16 [32, 2048, 128, 128], P('group', 'memory'), may hold values from -6 to 6
- candidates: int32 [32, 128, 64], P('group', 'memory'), may hold values from 0 to 2047, as said below
- counts: int32 [32, 128], P('group', 'memory'), may hold values from 16 to 32
Outputs:
- batch_scores: float32 [32, 128, 256], P('group', 'memory')
- memory_scores: float32 [32, 128, 64], P('group', 'memory')
- loss: float32 [32, 128], P('group', 'memory')
Inputs may be any that keep to these rules, and one draw needn't show every extreme that they name: `candidates`: passage id r of a column lies on memory index r // 128. Among the valid slots of the queries of one device (queries[g, m * 8 to (m + 1) * 8 - 1]), at most 24 name passages of any one memory index, and some memory index is named by exactly 24 of them. Ids may repeat.
All inputs are finite; a program needn't handle non-finite values.
Results may differ from a plain program's by a relative error of at most 0.0003.
Values may be sent and summed in bfloat16 or wider, within the bound.
A program may use at most 128 MiB of HBM per device.

v0:
```python
import math

import jax
import jax.numpy as jnp
from jax import lax
from jax.sharding import PartitionSpec as P


def sim_block(rows, key_flat, tokens, width):
    product = lax.dot_general(
        rows, key_flat, (((1,), (1,)), ((), ())), preferred_element_type=jnp.float32
    )
    product = product.reshape(rows.shape[0] // tokens, tokens, key_flat.shape[0] // width, width)
    return jnp.sum(jnp.max(product, axis=3), axis=1)


def pair_scores(query_rows, passages):
    product = jnp.einsum("nqd,nsd->nqs", query_rows, passages, preferred_element_type=jnp.float32)
    return jnp.sum(jnp.max(product, axis=2), axis=1)


def body(queries, positives, memory, candidates, counts):
    q_count = queries.shape[1]
    q_tokens = queries.shape[2]
    width = queries.shape[3]
    p_tokens = positives.shape[2]
    p_local = memory.shape[1]
    slots_per = candidates.shape[2]
    shards = lax.axis_size("memory")
    groups = lax.axis_size("group")
    own_queries = queries[0]
    pos_flat = positives[0].reshape(q_count * p_tokens, width)
    piece = lax.all_gather(queries, "group", axis=0, tiled=True)
    count_rows = piece.shape[0] * piece.shape[1]
    step_size = math.gcd(count_rows, 16)
    grouped = piece.reshape(count_rows // step_size, step_size * q_tokens, width)
    result = lax.map(
        lambda block_rows: sim_block(block_rows, pos_flat, q_tokens, p_tokens), grouped
    )
    table = result.reshape(piece.shape[0], piece.shape[1], q_count)
    batch_scores = lax.all_to_all(table, "group", split_axis=0, concat_axis=2, tiled=True)
    valid = lax.broadcasted_iota(jnp.int32, (q_count, slots_per), 1) < counts[0][:, None]
    total = q_count * slots_per
    capacity = 3 * (slots_per // 2) * q_count // (2 * shards)
    valid_flat = valid.reshape(total)
    owner_flat = (candidates[0] // p_local).reshape(total)
    local_flat = (candidates[0] % p_local).reshape(total)
    onehot = jnp.where(
        valid_flat[:, None],
        (owner_flat[:, None] == jnp.arange(shards, dtype=jnp.int32)[None, :]).astype(jnp.int32),
        0,
    )
    before = jnp.cumsum(onehot, axis=0) - onehot
    ranks = jnp.sum(before * onehot, axis=1)
    slot_ids = jnp.where(valid_flat, owner_flat * capacity + ranks, shards * capacity)
    query_ids = lax.broadcasted_iota(jnp.int32, (q_count, slots_per), 0).reshape(total)
    request = (
        jnp.zeros((shards * capacity + 1,), jnp.int32)
        .at[slot_ids]
        .set(local_flat)[:-1]
        .reshape(shards, capacity)
    )
    asker = (
        jnp.zeros((shards * capacity + 1,), jnp.int32)
        .at[slot_ids]
        .set(query_ids)[:-1]
        .reshape(shards, capacity)
    )
    incoming = lax.all_to_all(request, "memory", split_axis=0, concat_axis=0, tiled=True)
    blocks = memory[0][incoming]
    arrived = lax.all_to_all(blocks, "memory", split_axis=0, concat_axis=0, tiled=True)
    rows = own_queries[asker.reshape(shards * capacity)]
    slot_scores = pair_scores(rows, arrived.reshape(shards * capacity, p_tokens, width))
    picked = slot_scores[jnp.minimum(slot_ids, shards * capacity - 1)].reshape(q_count, slots_per)
    memory_scores = jnp.where(valid, picked, 0.0)
    batch_rows = batch_scores[0]
    top = jnp.maximum(
        jnp.max(batch_rows, axis=1), jnp.max(jnp.where(valid, picked, -jnp.inf), axis=1)
    )
    total_exp = jnp.sum(jnp.exp(batch_rows - top[:, None]), axis=1) + jnp.sum(
        jnp.where(valid, jnp.exp(picked - top[:, None]), 0.0), axis=1
    )
    own_index = lax.axis_index("group") * q_count + jnp.arange(q_count, dtype=jnp.int32)
    batch_iota = jnp.arange(groups * q_count, dtype=jnp.int32)
    target = jnp.sum(jnp.where(batch_iota[None, :] == own_index[:, None], batch_rows, 0.0), axis=1)
    losses = top + jnp.log(total_exp) - target
    return (batch_scores, memory_scores[None], losses[None])


def solution(mesh):
    in_specs = (
        P("group", "memory", None, None),
        P("group", "memory", None, None),
        P("group", "memory", None, None),
        P("group", "memory", None),
        P("group", "memory"),
    )
    out_specs = (P("group", "memory", None), P("group", "memory", None), P("group", "memory"))
    return jax.shard_map(body, mesh=mesh, in_specs=in_specs, out_specs=out_specs, check_vma=False)
```

profile of v0, /device:TPU:1, one launch (start us, length us, event | category | flops | bytes accessed | tf_op | source)
XLA Modules:
  0.0 717.0 jit_solution(6732661477595397931)
XLA Ops:
  7.9 0.8 squeeze.19
  11.6 1.3 reduce.10
  13.3 1.2 reduce-window.6
  14.8 2.4 scatter_custom_fusion.1
  18.0 15.7 %all-to-all-start.1 = ((s32[16,1,24]{2,1,0:T(1,128)}), s32[16,1,24]{2,1,0:T(1,128)S(1)}, u32[]{:S(2)}, u32[]{:S(2)}) async-start(s32[16,1,24]{2,1,0:T(1,128)} %all_to_all.28), calls=%async_computation.1 | async-start | bytes 16384 | tf_op jit(solution)/shard_map/all_to_all | solution.py:69
  33.8 11.2 %all-to-all-done.1 = s32[16,1,24]{2,1,0:T(1,128)S(1)} async-done(((s32[16,1,24]{2,1,0:T(1,128)}), s32[16,1,24]{2,1,0:T(1,128)S(1)}, u32[]{:S(2)}, u32[]{:S(2)}) %all-to-all-start.1) | async-done | bytes 1568 | tf_op jit(solution)/shard_map/all_to_all | solution.py:69
  45.1 31.0 %all-gather.2.cloned.1.call-done = bf16[32,8,32,128]{3,2,1,0:T(8,128)(2,1)} async-done(((bf16[1,8,32,128]{3,2,1,0:T(8,128)(2,1)}), bf16[32,8,32,128]{3,2,1,0:T(8,128)(2,1)}) %all-gather.2.cloned.1.call-update) | async-done | bytes 2097168 | tf_op jit(solution)/shard_map/all_gather | solution.py:33
  76.0 46.0 %while.10 = (s32[]{:T(128)}, f32[16,16,8]{1,0,2:T(8,128)S(1)}, bf16[16,512,128]{2,1,0:T(8,128)(2,1)}, bf16[1024,128]{1,0:T(8,128)(2,1)}, s32[]{:T(128)}, /*index=5*/f32[]{:T(128)}, s32[]{:T(128)}) while((s32[]{:T(128)}, f32[16,16,8]{1,0,2:T(8,128)S(1)}, bf16[16,512,128]{2,1,0:T(8,128)(2,1)}, bf16[1024,128]{1,0:T(8,128)(2,1)}, s32[]{:T(128)}, ...), condition=%wide.region_3.4_spmd, body=%wide.region_0.3_spmd.sunk | while | flops 134741888 | bytes 690777 | solution.py:37
  76.0 0.9 constant_dynamic-slice_fusion.2
  77.0 1.7 convolution_reduce_fusion.3
  78.9 0.9 constant_dynamic-slice_fusion.2
  79.8 1.7 convolution_reduce_fusion.3
  81.8 0.9 constant_dynamic-slice_fusion.2
  82.7 1.7 convolution_reduce_fusion.3
  84.7 0.9 constant_dynamic-slice_fusion.2
  85.6 1.7 convolution_reduce_fusion.3
  87.5 0.9 constant_dynamic-slice_fusion.2
  88.5 1.7 convolution_reduce_fusion.3
  90.4 0.9 constant_dynamic-slice_fusion.2
  91.3 1.7 convolution_reduce_fusion.3
  93.3 0.9 constant_dynamic-slice_fusion.2
  94.2 1.7 convolution_reduce_fusion.3
  96.2 0.9 constant_dynamic-slice_fusion.2
  97.1 1.7 convolution_reduce_fusion.3
  99.0 0.9 constant_dynamic-slice_fusion.2
  100.0 1.7 convolution_reduce_fusion.3
  101.9 0.9 constant_dynamic-slice_fusion.2
  102.8 1.7 convolution_reduce_fusion.3
  104.8 0.9 constant_dynamic-slice_fusion.2
  105.7 1.7 convolution_reduce_fusion.3
  107.7 0.9 constant_dynamic-slice_fusion.2
  108.6 1.7 convolution_reduce_fusion.3
  110.5 0.9 constant_dynamic-slice_fusion.2
  111.5 1.7 convolution_reduce_fusion.3
  113.4 0.9 constant_dynamic-slice_fusion.2
  114.3 1.7 convolution_reduce_fusion.3
  116.3 0.9 constant_dynamic-slice_fusion.2
  117.2 1.7 convolution_reduce_fusion.3
  119.2 0.9 constant_dynamic-slice_fusion.2
  120.1 1.7 convolution_reduce_fusion.3
  122.9 5.1 all-to-all-start
  128.0 13.3 %gather_fusion.1 = bf16[384,128,128]{2,1,0:T(8,128)(2,1)} fusion(bf16[128,128,128]{2,1,0:T(8,128)(2,1)} %bitcast.69, s32[1024]{0:T(1024)S(1)} %pad_clamp_fusion.1), kind=kCustom, calls=%fused_computation.1 | custom fusion | bytes 25167360 | tf_op jit(solution)/shard_map/gather | solution.py:70
  141.3 12.2 %all-to-all-start.2 = ((bf16[16,24,128,128]{3,2,1,0:T(8,128)(2,1)}), bf16[16,24,128,128]{3,2,1,0:T(8,128)(2,1)}, u32[]{:S(2)}, u32[]{:S(2)}) async-start(bf16[16,24,128,128]{3,2,1,0:T(8,128)(2,1)} %bitcast.68), calls=%async_computation.2 | async-start | bytes 25165824 | tf_op jit(solution)/shard_map/all_to_all | solution.py:71
  153.6 2.4 scatter_custom_fusion
  156.1 2.4 gather_fusion
  159.3 535.6 %all-to-all-done.2 = bf16[16,24,128,128]{3,2,1,0:T(8,128)(2,1)} async-done(((bf16[16,24,128,128]{3,2,1,0:T(8,128)(2,1)}), bf16[16,24,128,128]{3,2,1,0:T(8,128)(2,1)}, u32[]{:S(2)}, u32[]{:S(2)}) %all-to-all-start.2) | async-done | bytes 12582944 | tf_op jit(solution)/shard_map/all_to_all | solution.py:71
  694.9 9.7 %convolution_reduce_fusion.1 = f32[384,32]{1,0:T(8,128)S(1)} fusion(bf16[384,32,128]{2,1,0:T(8,128)(2,1)S(1)} %gather_fusion, bf16[384,128,128]{2,1,0:T(8,128)(2,1)} %bitcast.19), kind=kOutput, calls=%fused_computation.7 | convolution fusion | flops 404213760 | bytes 15777792 | tf_op jit(solution)/shard_map/nqd,nsd->nqs/dot_general | solution.py:18
  704.8 3.5 gather_fusion.2
  (101 shorter events, 11.8 us)
Async XLA Ops:
  7.2 68.9 %all-gather.2.cloned.1.call-start = ((), (), s32[]{:S(2)}) async-start(), calls=%async_computation.3 | async-start | bytes 2162688 | tf_op jit(solution)/shard_map/all_gather | solution.py:33
  18.0 27.0 %all-to-all-start.1 = ((s32[16,1,24]{2,1,0:T(1,128)}), s32[16,1,24]{2,1,0:T(1,128)S(1)}, u32[]{:S(2)}, u32[]{:S(2)}) async-start(s32[16,1,24]{2,1,0:T(1,128)} %all_to_all.28), calls=%async_computation.1 | async-start | bytes 16384 | tf_op jit(solution)/shard_map/all_to_all | solution.py:69
  122.9 18.4 %all-to-all-start = ((f32[32,8,8]{1,2,0:T(8,128)}), f32[32,8,8]{1,2,0:T(8,128)S(1)}, u32[]{:S(2)}, u32[]{:S(2)}) async-start(f32[32,8,8]{1,2,0:T(8,128)} %copy.27), calls=%async_computation | async-start | bytes 262144 | tf_op jit(solution)/shard_map/all_to_all | solution.py:41
  141.3 14.8 %copy-start = (bf16[1,8,32,128]{3,2,1,0:T(8,128)(2,1)S(1)}, bf16[1,8,32,128]{3,2,1,0:T(8,128)(2,1)}, u32[]{:S(2)}) copy-start(bf16[1,8,32,128]{3,2,1,0:T(8,128)(2,1)} %param.7) | copy-start | bytes 196612
  141.3 553.6 %all-to-all-start.2 = ((bf16[16,24,128,128]{3,2,1,0:T(8,128)(2,1)}), bf16[16,24,128,128]{3,2,1,0:T(8,128)(2,1)}, u32[]{:S(2)}, u32[]{:S(2)}) async-start(bf16[16,24,128,128]{3,2,1,0:T(8,128)(2,1)} %bitcast.68), calls=%async_computation.2 | async-start | bytes 25165824 | tf_op jit(solution)/shard_map/all_to_all | solution.py:71
  694.9 13.5 %copy-start.1 = (s32[1,8]{1,0:T(1,128)S(1)}, s32[1,8]{1,0:T(1,128)}, u32[]{:S(2)}) copy-start(s32[1,8]{1,0:T(1,128)} %param.11) | copy-start | bytes 100
Sparse Core Ops, SparseCore 0:
  11.1 64.8 all-gather.1
where the time goes:
time: 719 us; the launch traced here: 717 us
  waiting for transfers between devices  578 us (80%)
  local copies, waits for them, and re-layouts  46.4 us (6%)
  matrix products  37.4 us (5%)
  starting transfers between devices  33.1 us (5%)
  between operations  14.2 us (2%)
    all_to_all x1, waiting for transfers between devices, body(): lax.all_to_all(blocks, 'memory', split_axis=0, concat_axis=0, tiled=True)  536 us
    all_gather x1, waiting for transfers between devices, body(): piece = lax.all_gather(queries, 'group', axis=0, tiled=True)  31 us
    dot_general x16, matrix products, sim_block(): lax.dot_general(rows, key_flat, (((1,), (1,)), ((), ())), preferred_eleme...  27.7 us
    all_to_all x1, starting transfers between devices, body(): lax.all_to_all(request, 'memory', split_axis=0, concat_axis=0, tiled=True)  15.7 us
    dynamic_slice x16, local copies, waits for them, and re-layouts, body(): lax.map(lambda block_rows: sim_block(block_rows, pos_flat, q_tokens, p_to...  14.7 us
  transfers between devices with their start and end apart: 4, of which 3 were waited for; matrix products, arithmetic and copies ran while one was open for 4% of the time, Pallas kernels for 0%

commit v1 on v0

v1 whole, which is shorter than its diff:
```python
import functools
import math

import jax
import jax.numpy as jnp
from jax import lax
from jax.experimental import pallas as pl
from jax.experimental.pallas import tpu as pltpu
from jax.sharding import PartitionSpec as P

MESH = pl.DeviceIdType.MESH
F32 = jnp.float32
BF16 = jnp.bfloat16
I32 = jnp.int32
CAP = 24
Q = 8
TOK = 32
LIVE = 32
LANES = 128
COLS = Q * TOK


def iota(shape, axis):
    return lax.broadcasted_iota(I32, shape, axis)


def kernel(zs, side, q_hbm, pos_hbm, mem_hbm, cand_ref, cnt_ref, out_b, out_m, out_l,
           qv, posv, memv, zbuf, gbuf, ask_out, ask_in, ids, row_out, row_in, tile_out, tile_in,
           load_sem, zr_sem, zl_sem, cls_sem, sib_sem, ask_sem, row_sem, tile_sem,
           zsend_sem, gsend_sem, ask_send_sem, row_send_sem, tile_send_sem):
    half = zs // 2
    plane = side * side
    ng = 2 * plane
    items = zs - 1
    feat = LANES // 2

    z = lax.axis_index("memory")
    g = lax.axis_index("group")
    core = lax.rem(g, 2)
    px = lax.rem(g // 2, side)
    py = g // (2 * side)
    z_right = lax.rem(z + 1, zs)
    z_left = lax.rem(z + zs - 1, zs)
    sibling = g + 1 - 2 * core

    def source(k, c):
        a = lax.rem(k, side)
        b = k // side
        dx = a + c * (b - a)
        dy = b + c * (a - b)
        return (lax.rem(py - dy + side, side) * side + lax.rem(px - dx + side, side)) * 2 + c

    def target(a, b):
        dx = a + core * (b - a)
        dy = b + core * (a - b)
        return (lax.rem(py + dy, side) * side + lax.rem(px + dx, side)) * 2 + core

    load_q = pltpu.make_async_copy(q_hbm, qv, load_sem.at[0])
    load_q.start()
    load_pos = pltpu.make_async_copy(pos_hbm, posv, load_sem.at[1])
    load_mem = pltpu.make_async_copy(mem_hbm, memv, load_sem.at[2])
    load_pos.start()
    load_mem.start()

    barrier = pltpu.get_barrier_semaphore()

    def greet_z(i, _):
        pl.semaphore_signal(barrier, inc=1, device_id=(lax.rem(z + i, zs), g), device_id_type=MESH)
        return 0

    def greet_g(i, _):
        pl.semaphore_signal(barrier, inc=1, device_id=(z, lax.rem(g + i, ng)), device_id_type=MESH)
        return 0

    lax.fori_loop(1, zs, greet_z, 0)
    lax.fori_loop(1, ng, greet_g, 0)

    lane = iota((1, LANES), 1)
    cand = jnp.concatenate([cand_ref[...], jnp.zeros((Q, LANES - cand_ref.shape[1]), I32)], axis=1)
    parts, limits = [], []
    for h in range(2):
        flat = jnp.zeros((1, LANES), I32)
        limit = jnp.zeros((1, LANES), I32)
        for j in range(4):
            row = cand[4 * h + j : 4 * h + j + 1]
            if j:
                row = pltpu.roll(row, j * LIVE, 1)
            flat = jnp.where(lane // LIVE == j, row, flat)
            limit = jnp.where(lane // LIVE == j, cnt_ref[0, 4 * h + j], limit)
        parts.append(flat)
        limits.append(limit)
    flat = jnp.concatenate(parts, axis=1)
    limit = jnp.concatenate(limits, axis=1)
    slot = iota((1, COLS), 1)
    live = (slot % LIVE) < limit
    holds = LANES
    owner = jnp.where(live, flat // holds, -1)
    local = (flat % holds).astype(F32)
    query = (slot // LIVE).astype(F32)
    onehot = jnp.where(iota((zs, COLS), 0) == owner, 1.0, 0.0).astype(F32)
    upper = jnp.where(iota((COLS, COLS), 0) < iota((COLS, COLS), 1), 1.0, 0.0).astype(BF16)
    before = jnp.dot(onehot.astype(BF16), upper, preferred_element_type=F32)
    rank = jnp.sum(onehot * before, axis=0, keepdims=True)
    place = (iota((LANES, COLS), 0).astype(F32) == rank)
    both = jnp.concatenate([onehot * local, onehot * query], axis=0).astype(BF16)
    table = lax.dot_general(
        both, jnp.where(place, 1.0, 0.0).astype(BF16), (((1,), (1,)), ((), ())), preferred_element_type=F32
    )
    code = (table[:zs] + 128.0 * table[zs:]).astype(I32)
    for o in range(zs):
        ask_out[o] = code[o : o + 1]

    load_q.wait()
    turned = qv[...].astype(F32).T.astype(BF16)
    zbuf[z] = turned
    gbuf[g] = turned
    ask_in[z] = ask_out[z]

    pl.semaphore_wait(barrier, zs - 1 + ng - 1)

    def piece(i):
        return i // 2 + 1, lax.rem(i, 2) * feat

    def z_copy(block, first, sem, to):
        ref = zbuf.at[block, pl.ds(pl.multiple_of(first, feat), feat)]
        return pltpu.make_async_remote_copy(
            src_ref=ref, dst_ref=ref, send_sem=zsend_sem, recv_sem=sem,
            device_id=(to, g), device_id_type=MESH,
        )

    def right_send(i):
        d, first = piece(i)
        return z_copy(lax.rem(z - d + 1 + zs, zs), first, zr_sem.at[i], z_right)

    def left_send(i):
        d, first = piece(i)
        first = jnp.where(i == items - 1, feat, first)
        return z_copy(lax.rem(z + d - 1, zs), first, zl_sem.at[i], z_left)

    def right_wait(i):
        d, first = piece(i)
        z_copy(lax.rem(z - d + zs, zs), first, zr_sem.at[i], z_right).wait_recv()

    def left_wait(i):
        d, first = piece(i)
        first = jnp.where(i == items - 1, feat, first)
        z_copy(lax.rem(z + d, zs), first, zl_sem.at[i], z_left).wait_recv()

    def g_copy(block, sem, to):
        ref = gbuf.at[block]
        return pltpu.make_async_remote_copy(
            src_ref=ref, dst_ref=ref, send_sem=gsend_sem, recv_sem=sem,
            device_id=(z, to), device_id_type=MESH,
        )

    for i in range(min(2, items)):
        right_send(jnp.int32(i)).start()
        left_send(jnp.int32(i)).start()
    for a in range(1, side):
        g_copy(g, cls_sem.at[a], target(a, 0)).start()
    g_copy(g, sib_sem.at[0], sibling).start()
    for b in range(1, side):
        g_copy(g, cls_sem.at[b * side], target(0, b)).start()

    def ask(i, _):
        to = lax.rem(z + i, zs)
        pltpu.make_async_remote_copy(
            src_ref=ask_out.at[to], dst_ref=ask_in.at[z], send_sem=ask_send_sem, recv_sem=ask_sem,
            device_id=(to, g), device_id_type=MESH,
        ).start()
        return 0

    lax.fori_loop(1, zs, ask, 0)

    def best(passages, tokens):
        r = jnp.dot(passages, tokens, preferred_element_type=F32)
        return jnp.max(r.reshape(passages.shape[0] // LANES, LANES, COLS), axis=1)

    lane8 = iota((8, LANES), 1)

    def batch(block):
        m = best(posv[...], gbuf[block])
        x0, x1 = m[:, :LANES], m[:, LANES:]
        x0 = x0 + pltpu.roll(x0, LANES - 16, 1)
        x1 = x1 + pltpu.roll(x1, LANES - 16, 1)
        x = jnp.where(lane8 % 32 < 16, x0, pltpu.roll(x1, 16, 1))
        for s in (8, 4, 2, 1):
            x = x + pltpu.roll(x, LANES - s, 1)
        return x

    def batch_send(block):
        tile_out[block] = batch(block)
        pltpu.make_async_remote_copy(
            src_ref=tile_out.at[block], dst_ref=tile_in.at[g], send_sem=tile_send_sem, recv_sem=tile_sem,
            device_id=(z, block), device_id_type=MESH,
        ).start()

    diag = iota((CAP, LANES), 0) == iota((CAP, LANES), 1)
    col_query = iota((CAP, COLS), 1) // TOK

    def memory_rows(asker):
        tokens = zbuf[asker]
        rows = []
        for first in range(0, CAP, 8):
            passages = jnp.concatenate([memv[ids[asker, 0, first + j] & (holds - 1)] for j in range(8)], axis=0)
            rows.append(best(passages, tokens))
        m = jnp.concatenate(rows, axis=0)
        asked = jnp.sum(jnp.where(diag, ask_in[asker].astype(F32), 0.0), axis=1, keepdims=True)
        asked = asked.astype(I32) // holds
        s = jnp.sum(jnp.where(col_query == asked, m, 0.0), axis=1, keepdims=True)
        return jnp.sum(jnp.where(diag, s, 0.0), axis=0, keepdims=True)

    def memory_send(asker):
        row_out[asker] = memory_rows(asker)
        pltpu.make_async_remote_copy(
            src_ref=row_out.at[asker], dst_ref=row_in.at[z], send_sem=row_send_sem, recv_sem=row_sem,
            device_id=(asker, g), device_id_type=MESH,
        ).start()

    load_pos.wait()
    tile_in[g] = batch(g)

    for a in range(1, side):
        k = jnp.int32(a)
        block = source(k, core)
        g_copy(block, cls_sem.at[a], sibling).wait_recv()
        g_copy(block, sib_sem.at[a], sibling).start()
        for b in range(1, side):
            g_copy(block, cls_sem.at[b * side + a], target(0, b)).start()

    pltpu.make_async_copy(ask_in.at[pl.ds(0, zs - 1)], ask_in.at[pl.ds(0, zs - 1)], ask_sem).wait()
    load_ids = pltpu.make_async_copy(ask_in, ids, load_sem.at[3])
    load_ids.start()
    load_ids.wait()
    load_mem.wait()
    row_in[z] = memory_rows(z)

    def step(t, _):
        right_wait(t)

        @pl.when(t + 2 <= items - 1)
        def _():
            right_send(t + 2).start()

        left_wait(t)

        @pl.when(t + 2 <= items - 2)
        def _():
            left_send(t + 2).start()

        @pl.when(t == items - 2)
        def _():
            left_send(t + 1).start()

        k = t + 1
        block = source(k, core)

        @pl.when(k >= side)
        def _():
            g_copy(block, cls_sem.at[k], sibling).wait_recv()
            g_copy(block, sib_sem.at[k], sibling).start()

        other = source(t, 1 - core)
        g_copy(other, sib_sem.at[t], sibling).wait_recv()

        @pl.when(t > 0)
        def _():
            d = (t + 1) // 2
            odd = lax.rem(t, 2)
            memory_send(jnp.where(odd == 1, lax.rem(z - d + zs, zs), lax.rem(z + d, zs)))

        batch_send(block)
        batch_send(other)
        return 0

    lax.fori_loop(0, items, step, 0)

    memory_send(lax.rem(z + half, zs))
    last = source(jnp.int32(items), 1 - core)
    g_copy(last, sib_sem.at[items], sibling).wait_recv()
    batch_send(last)

    pltpu.make_async_copy(row_in.at[pl.ds(0, zs - 1)], row_in.at[pl.ds(0, zs - 1)], row_sem).wait()
    got = jnp.concatenate([row_in[o] for o in range(zs)], axis=0)
    spread = lax.dot_general(
        got, onehot, (((0,), (0,)), ((), ())), preferred_element_type=F32, precision=lax.Precision.HIGHEST
    )
    picked = jnp.sum(jnp.where(place, spread, 0.0), axis=0, keepdims=True)
    sub8 = iota((Q, LANES), 0)
    scores = jnp.zeros((Q, LANES), F32)
    count = jnp.zeros((Q, LANES), I32)
    for q in range(Q):
        h, j = q // 4, q % 4
        row = picked[:, h * LANES : (h + 1) * LANES]
        if j:
            row = pltpu.roll(row, LANES - j * LIVE, 1)
        scores = jnp.where(sub8 == q, row, scores)
        count = jnp.where(sub8 == q, cnt_ref[0, q], count)
    valid = lane8 < count
    scores = jnp.where(valid, scores, 0.0)
    out_m[...] = scores[:, : out_m.shape[1]]

    pltpu.make_async_copy(tile_in.at[pl.ds(0, ng - 1)], tile_in.at[pl.ds(0, ng - 1)], tile_sem).wait()
    turned_scores = tile_in[...].reshape(ng * 8, LANES).T
    order = [0, 32, 64, 96, 16, 48, 80, 112]
    rows = jnp.concatenate([turned_scores[o : o + 1] for o in order], axis=0)
    out_b[...] = rows
    top = jnp.maximum(
        jnp.max(rows, axis=1, keepdims=True),
        jnp.max(jnp.where(valid, scores, -jnp.inf), axis=1, keepdims=True),
    )
    total = jnp.sum(jnp.exp(rows - top), axis=1, keepdims=True) + jnp.sum(
        jnp.where(valid, jnp.exp(scores - top), 0.0), axis=1, keepdims=True
    )
    mine = iota(rows.shape, 1) == g * Q + iota(rows.shape, 0)
    own = jnp.sum(jnp.where(mine, rows, 0.0), axis=1, keepdims=True)
    loss = top + jnp.log(total) - own
    spread_loss = jnp.where(lane8 == sub8, loss, 0.0)
    out_l[...] = jnp.sum(spread_loss, axis=0, keepdims=True)[:, :Q]

    pltpu.make_async_copy(zbuf.at[pl.ds(0, items)], zbuf.at[pl.ds(0, items)], zsend_sem).wait()
    pltpu.make_async_copy(gbuf.at[pl.ds(0, ng - 1)], gbuf.at[pl.ds(0, ng - 1)], gsend_sem).wait()
    pltpu.make_async_copy(ask_in.at[pl.ds(0, items)], ask_in.at[pl.ds(0, items)], ask_send_sem).wait()
    pltpu.make_async_copy(row_in.at[pl.ds(0, items)], row_in.at[pl.ds(0, items)], row_send_sem).wait()
    pltpu.make_async_copy(tile_in.at[pl.ds(0, ng - 1)], tile_in.at[pl.ds(0, ng - 1)], tile_send_sem).wait()


def body(queries, positives, memory, candidates, counts):
    zs = lax.axis_size("memory")
    ng = lax.axis_size("group")
    side = math.isqrt(ng // 2)
    assert ng == 2 * side * side and zs == side * side
    width = queries.shape[3]
    p_local = memory.shape[1]
    any_space = pl.BlockSpec(memory_space=pl.ANY)
    vmem = pl.BlockSpec(memory_space=pltpu.VMEM)
    smem = pl.BlockSpec(memory_space=pltpu.SMEM)
    dma = pltpu.SemaphoreType.DMA
    slots = candidates.shape[2]
    out_b, out_m, out_l = pl.pallas_call(
        functools.partial(kernel, zs, side),
        out_shape=(
            jax.ShapeDtypeStruct((Q, ng * Q), F32),
            jax.ShapeDtypeStruct((Q, slots), F32),
            jax.ShapeDtypeStruct((1, Q), F32),
        ),
        in_specs=[any_space, any_space, any_space, vmem, smem],
        out_specs=(vmem, vmem, vmem),
        scratch_shapes=[
            pltpu.VMEM((COLS, width), BF16),
            pltpu.VMEM((Q * LANES, width), BF16),
            pltpu.VMEM((p_local, LANES, width), BF16),
            pltpu.VMEM((zs, width, COLS), BF16),
            pltpu.VMEM((ng, width, COLS), BF16),
            pltpu.VMEM((zs, 1, LANES), I32),
            pltpu.VMEM((zs, 1, LANES), I32),
            pltpu.SMEM((zs, 1, LANES), I32),
            pltpu.VMEM((zs, 1, LANES), F32),
            pltpu.VMEM((zs, 1, LANES), F32),
            pltpu.VMEM((ng, 8, LANES), F32),
            pltpu.VMEM((ng, 8, LANES), F32),
            dma((4,)), dma((zs - 1,)), dma((zs - 1,)), dma((ng // 2,)), dma((ng // 2,)),
            dma, dma, dma,
            dma, dma, dma, dma, dma,
        ],
        compiler_params=pltpu.CompilerParams(
            collective_id=0, has_side_effects=True, vmem_limit_bytes=40 * 1024 * 1024
        ),
        cost_estimate=pl.CostEstimate(flops=5 * 10**9, bytes_accessed=5 * 10**6, transcendentals=4096),
        name="scores",
    )(
        queries[0].reshape(COLS, width),
        positives[0].reshape(Q * LANES, width),
        memory[0],
        candidates[0],
        counts,
    )
    return out_b[None], out_m[None], out_l


def solution(mesh):
    in_specs = (
        P("group", "memory", None, None),
        P("group", "memory", None, None),
        P("group", "memory", None, None),
        P("group", "memory", None),
        P("group", "memory"),
    )
    out_specs = (P("group", "memory", None), P("group", "memory", None), P("group", "memory"))
    return jax.shard_map(body, mesh=mesh, in_specs=in_specs, out_specs=out_specs, check_vma=False)
```

time: 719 us -> 76.1 us (0.11)
  waiting for transfers between devices: 578 us -> 0 us
  Pallas kernels: 0 us -> 67.9 us
  local copies, waits for them, and re-layouts: 46.4 us -> 7.01 us
  matrix products: 37.4 us -> 0 us
  starting transfers between devices: 33.1 us -> 0 us
  between operations: 14.2 us -> 0.65 us
    all_to_all x3 -> x0, waiting for transfers between devices: 547 us -> none  [the longest x1 536 us: body(): lax.all_to_all(blocks, 'memory', split_axis=0, concat_axis=0, tiled=True)]
    pallas_call x0 -> x1, Pallas kernels: none -> 67.9 us  [body(): pl.pallas_call(functools.partial(kernel, zs, side), out_shape=(jax.ShapeD...]
    dot_general x17 -> x0, matrix products: 37.4 us -> none  [the longest x16 27.7 us: sim_block(): lax.dot_general(rows, key_flat, (((1,), (1,)), ((), ())), preferred_eleme...]
    all_to_all x3 -> x0, starting transfers between devices: 33 us -> none  [the longest x1 15.7 us: body(): lax.all_to_all(request, 'memory', split_axis=0, concat_axis=0, tiled=True)]
    all_gather x1 -> x0, waiting for transfers between devices: 31 us -> none  [body(): piece = lax.all_gather(queries, 'group', axis=0, tiled=True)]
    gather x3 -> x0, local copies, waits for them, and re-layouts: 19.3 us -> none  [the longest x1 13.3 us: body(): blocks = memory[0][incoming]]
    dynamic_slice x16 -> x0, local copies, waits for them, and re-layouts: 14.7 us -> none  [body(): lax.map(lambda block_rows: sim_block(block_rows, pos_flat, q_tokens, p_to...]
  transfers between devices with their start and end apart: 4 -> 0, of which waited for: 3 -> 0; matrix products, arithmetic and copies ran while one was open for 4% -> 0% of each run, Pallas kernels for 0% -> 0%
where the time goes in v1:
time: 76.1 us; the launch traced here: 75.6 us
  Pallas kernels  67.9 us (89%)
  local copies, waits for them, and re-layouts  7.01 us (9%)
    pallas_call x1, Pallas kernels, body(): pl.pallas_call(functools.partial(kernel, zs, side), out_shape=(jax.ShapeD...  67.9 us
    unnamed x13, local copies, waits for them, and re-layouts  7.01 us

profile of v1, /device:TPU:1, one launch (start us, length us, event | category | flops | bytes accessed | tf_op | source)
XLA Modules:
  0.0 75.6 jit_solution(169577331255341042)
XLA Ops:
  0.6 0.0 copy-start
  0.6 2.2 %copy-done = bf16[1,128,128,128]{3,2,1,0:T(8,128)(2,1)S(1)} copy-done((bf16[1,128,128,128]{3,2,1,0:T(8,128)(2,1)S(1)}, bf16[1,128,128,128]{3,2,1,0:T(8,128)(2,1)}, u32[]{:S(2)}) %copy-start) | copy-done | bytes 4194328
  2.8 0.0 copy-start.1
  2.8 0.9 %copy-done.1 = bf16[1,8,128,128]{3,2,1,0:T(8,128)(2,1)S(1)} copy-done((bf16[1,8,128,128]{3,2,1,0:T(8,128)(2,1)S(1)}, bf16[1,8,128,128]{3,2,1,0:T(8,128)(2,1)}, u32[]{:S(2)}) %copy-start.1) | copy-done | bytes 262168
  3.8 0.0 copy-start.2
  3.8 0.8 %copy-done.2 = bf16[1,8,32,128]{3,2,1,0:T(8,128)(2,1)S(1)} copy-done((bf16[1,8,32,128]{3,2,1,0:T(8,128)(2,1)S(1)}, bf16[1,8,32,128]{3,2,1,0:T(8,128)(2,1)}, u32[]{:S(2)}) %copy-start.2) | copy-done | bytes 65560
  4.6 0.0 copy-start.3
  4.6 0.7 copy-done.3
  5.3 0.0 copy-start.4
  5.3 0.7 copy-done.4
  6.0 67.9 %scores.1 = (f32[8,256]{1,0:T(8,128)S(1)}, f32[8,64]{1,0:T(8,128)S(1)}, f32[1,8]{1,0:T(1,128)S(1)}) custom-call(bf16[256,128]{1,0:T(8,128)(2,1)S(1)} %bitcast.10, bf16[1024,128]{1,0:T(8,128)(2,1)S(1)} %bitcast.9, bf16[128,128,128]{2,1,0:T(8,128)(2,1)S(1)} %bitcast.8, s32[8,64]{1,0:T(8,128)S(1)} %bitcast.11, s32[1,8]{1,0:T(1,128)S(1)} %copy-done.4), custom_call_target="tpu_custom_call" | custom-call | flops 5000000000 | bytes 5000000 | tf_op jit(solution)/shard_map/scores/pallas_call | solution.py:340
  73.8 0.6 copy.11
  74.5 0.6 copy.12
  75.0 0.5 copy.13
Async XLA Ops:
  0.6 2.2 %copy-start = (bf16[1,128,128,128]{3,2,1,0:T(8,128)(2,1)S(1)}, bf16[1,128,128,128]{3,2,1,0:T(8,128)(2,1)}, u32[]{:S(2)}) copy-start(bf16[1,128,128,128]{3,2,1,0:T(8,128)(2,1)} %param.7) | copy-start | bytes 12582916
  2.8 0.9 %copy-start.1 = (bf16[1,8,128,128]{3,2,1,0:T(8,128)(2,1)S(1)}, bf16[1,8,128,128]{3,2,1,0:T(8,128)(2,1)}, u32[]{:S(2)}) copy-start(bf16[1,8,128,128]{3,2,1,0:T(8,128)(2,1)} %param.6) | copy-start | bytes 786436
  3.8 0.8 %copy-start.2 = (bf16[1,8,32,128]{3,2,1,0:T(8,128)(2,1)S(1)}, bf16[1,8,32,128]{3,2,1,0:T(8,128)(2,1)}, u32[]{:S(2)}) copy-start(bf16[1,8,32,128]{3,2,1,0:T(8,128)(2,1)} %param.5) | copy-start | bytes 196612
  4.6 0.7 copy-start.3
  5.3 0.7 copy-start.4

commit v2 on v1

v2 whole, which is shorter than its diff:
```python
import functools
import math

import jax
import jax.numpy as jnp
from jax import lax
from jax.experimental import pallas as pl
from jax.experimental.pallas import tpu as pltpu
from jax.sharding import PartitionSpec as P

MESH = pl.DeviceIdType.MESH
F32 = jnp.float32
BF16 = jnp.bfloat16
I32 = jnp.int32
CAP = 24
Q = 8
TOK = 32
LIVE = 32
LANES = 128
COLS = Q * TOK
CHUNKS = 4


def iota(shape, axis):
    return lax.broadcasted_iota(I32, shape, axis)


def kernel(zs, side, q_hbm, pos_hbm, mem_hbm, cand_ref, cnt_ref, out_b, out_m, out_l,
           qv, posv, memv, zbuf, gbuf, asks, ids, best_b, best_m, row_out, row_in, tile_out, tile_in,
           load_sem, zr_sem, zl_sem, ar_sem, al_sem, id_sem, cls_sem, sib_sem, row_sem, tile_sem,
           zsend_sem, asend_sem, gsend_sem, row_send_sem, tile_send_sem):
    half = zs // 2
    plane = side * side
    ng = 2 * plane
    side_bits = side.bit_length() - 1
    rows_of = LANES // CHUNKS

    z = lax.axis_index("memory")
    g = lax.axis_index("group")
    core = g & 1
    px = (g >> 1) & (side - 1)
    py = g >> (1 + side_bits)
    z_right = (z + 1) & (zs - 1)
    z_left = (z + zs - 1) & (zs - 1)
    sibling = g + 1 - 2 * core

    def source(k, c):
        a, b = k % side, k // side
        dx = a + c * (b - a)
        dy = b + c * (a - b)
        return (((py - dy) & (side - 1)) * side + ((px - dx) & (side - 1))) * 2 + c

    def target(a, b):
        dx = a + core * (b - a)
        dy = b + core * (a - b)
        return (((py + dy) & (side - 1)) * side + ((px + dx) & (side - 1))) * 2 + core

    def block_of(n):
        return source(n, core) if n < plane else source(n - plane, 1 - core)

    load_q = pltpu.make_async_copy(q_hbm, qv, load_sem.at[0])
    load_pos = pltpu.make_async_copy(pos_hbm, posv, load_sem.at[1])
    load_mem = pltpu.make_async_copy(mem_hbm, memv, load_sem.at[2])
    load_q.start()
    load_pos.start()
    load_mem.start()

    barrier = pltpu.get_barrier_semaphore()
    partners = [(z_right, g), (z_left, g), (z, sibling)]
    for a in range(1, side):
        partners += [(z, target(a, 0)), (z, target(0, a))]
    for to in partners:
        pl.semaphore_signal(barrier, inc=1, device_id=to, device_id_type=MESH)

    lane = iota((1, LANES), 1)
    cand = jnp.concatenate([cand_ref[...], jnp.zeros((Q, LANES - cand_ref.shape[1]), I32)], axis=1)
    parts, limits = [], []
    for h in range(2):
        flat = jnp.zeros((1, LANES), I32)
        limit = jnp.zeros((1, LANES), I32)
        for j in range(4):
            row = cand[4 * h + j : 4 * h + j + 1]
            if j:
                row = pltpu.roll(row, j * LIVE, 1)
            flat = jnp.where(lane >> 5 == j, row, flat)
            limit = jnp.where(lane >> 5 == j, cnt_ref[0, 4 * h + j], limit)
        parts.append(flat)
        limits.append(limit)
    flat = jnp.concatenate(parts, axis=1)
    limit = jnp.concatenate(limits, axis=1)
    slot = iota((1, COLS), 1)
    live = (slot & (LIVE - 1)) < limit
    owner = jnp.where(live, flat >> 7, -1)
    local = (flat & (LANES - 1)).astype(F32)
    query = (slot >> 5).astype(F32)
    onehot = jnp.where(iota((zs, COLS), 0) == owner, 1.0, 0.0).astype(F32)
    upper = jnp.where(iota((COLS, COLS), 0) < iota((COLS, COLS), 1), 1.0, 0.0).astype(BF16)
    before = jnp.dot(onehot.astype(BF16), upper, preferred_element_type=F32)
    rank = jnp.sum(onehot * before, axis=0, keepdims=True)
    place = iota((LANES, COLS), 0).astype(F32) == rank
    both = jnp.concatenate([onehot * local, onehot * query], axis=0).astype(BF16)
    table = lax.dot_general(
        both, jnp.where(place, 1.0, 0.0).astype(BF16), (((1,), (1,)), ((), ())), preferred_element_type=F32
    )
    code = (table[:zs] + 128.0 * table[zs:]).astype(I32)
    for o in range(zs // 2):
        asks[z, o] = code[2 * o : 2 * o + 1] + pltpu.roll(code[2 * o + 1 : 2 * o + 2], 64, 1)

    load_q.wait()
    turned = qv[...].astype(F32).T.astype(BF16)
    zbuf[z] = turned
    gbuf[g] = turned

    pl.semaphore_wait(barrier, len(partners))

    def ring_copy(ref, send, recv, to):
        return pltpu.make_async_remote_copy(
            src_ref=ref, dst_ref=ref, send_sem=send, recv_sem=recv, device_id=(to, g), device_id_type=MESH
        )

    def right(d, c, step):
        block = (z - d + step) & (zs - 1)
        ref = zbuf.at[block, pl.ds(c * rows_of, rows_of)]
        return ring_copy(ref, zsend_sem, zr_sem.at[(d - 1) * CHUNKS + c], z_right)

    def left(d, c, step):
        block = (z + d - step) & (zs - 1)
        ref = zbuf.at[block, pl.ds(c * rows_of, rows_of)]
        return ring_copy(ref, zsend_sem, zl_sem.at[(d - 1) * CHUNKS + c], z_left)

    def right_ask(d, step):
        return ring_copy(asks.at[(z - d + step) & (zs - 1)], asend_sem, ar_sem.at[d - 1], z_right)

    def left_ask(d, step):
        return ring_copy(asks.at[(z + d - step) & (zs - 1)], asend_sem, al_sem.at[d - 1], z_left)

    def by_right(d, c):
        return d < half or (d == half and c < CHUNKS // 2)

    def by_left(d, c):
        return d < half or (d == half and c >= CHUNKS // 2)

    def g_copy(block, sem, to):
        ref = gbuf.at[block]
        return pltpu.make_async_remote_copy(
            src_ref=ref, dst_ref=ref, send_sem=gsend_sem, recv_sem=sem,
            device_id=(z, to), device_id_type=MESH,
        )

    def asker_of(n):
        d = (n + 1) // 2
        return (z - d if n % 2 else z + d) & (zs - 1)

    def load_ids(n):
        return pltpu.make_async_copy(asks.at[asker_of(n), z >> 1], ids.at[n], id_sem.at[n])

    right_ask(1, 1).start()
    if half > 1:
        left_ask(1, 1).start()
    for c in range(CHUNKS):
        if by_right(1, c):
            right(1, c, 1).start()
        if by_left(1, c):
            left(1, c, 1).start()
    for a in range(1, side):
        g_copy(g, cls_sem.at[a], target(a, 0)).start()
    g_copy(g, sib_sem.at[0], sibling).start()
    for b in range(1, side):
        g_copy(g, cls_sem.at[b * side], target(0, b)).start()
    load_ids(0).start()

    def best(passages, tokens):
        r = jnp.dot(passages, tokens, preferred_element_type=F32)
        return jnp.max(r.reshape(passages.shape[0] // LANES, LANES, COLS), axis=1)

    lane8 = iota((8, LANES), 1)

    def batch_unit(n):
        best_b[n] = best(posv[...], gbuf[block_of(n)])

    def batch_finish(ns):
        for n in ns:
            x0, x1 = best_b[n, :, :LANES], best_b[n, :, LANES:]
            x0 = x0 + pltpu.roll(x0, LANES - 16, 1)
            x1 = x1 + pltpu.roll(x1, LANES - 16, 1)
            x = jnp.where((lane8 & 31) < 16, x0, pltpu.roll(x1, 16, 1))
            for s in (8, 4, 2, 1):
                x = x + pltpu.roll(x, LANES - s, 1)
            if n == 0:
                tile_in[g] = x
            else:
                tile_out[n] = x

    def batch_send(ns):
        for n in ns:
            if n:
                pltpu.make_async_remote_copy(
                    src_ref=tile_out.at[n], dst_ref=tile_in.at[g], send_sem=tile_send_sem, recv_sem=tile_sem,
                    device_id=(z, block_of(n)), device_id_type=MESH,
                ).start()

    diag = iota((CAP, LANES), 0) == iota((CAP, LANES), 1)
    col_query = iota((CAP, COLS), 1) >> 5
    upper_half = (z & 1) * 64

    def memory_unit(n, part):
        first = part * 8
        passages = jnp.concatenate(
            [memv[ids[n, 0, upper_half + first + j] & (LANES - 1)] for j in range(8)], axis=0
        )
        best_m[n, pl.ds(first, 8)] = best(passages, zbuf[asker_of(n)])

    def memory_finish(ns):
        for n in ns:
            row = asks[asker_of(n), z >> 1].astype(F32)
            row = jnp.where(upper_half > 0, pltpu.roll(row, 64, 1), row)
            asked = jnp.sum(jnp.where(diag, row, 0.0), axis=1, keepdims=True).astype(I32) >> 7
            s = jnp.sum(jnp.where(col_query == asked, best_m[n], 0.0), axis=1, keepdims=True)
            scores = jnp.sum(jnp.where(diag, s, 0.0), axis=0, keepdims=True)
            if n == 0:
                row_in[z] = scores
            else:
                row_out[n] = scores

    def memory_send(ns):
        for n in ns:
            if n:
                pltpu.make_async_remote_copy(
                    src_ref=row_out.at[n], dst_ref=row_in.at[z], send_sem=row_send_sem, recv_sem=row_sem,
                    device_id=(asker_of(n), g), device_id_type=MESH,
                ).start()

    turns = CHUNKS * (half - 1) + CHUNKS // 2
    moves = [[] for _ in range(turns + 4)]
    sums = [[] for _ in range(turns + 4)]

    def z_turn(d, c):
        def ask():
            right_ask(d, 0).wait_recv()
            if d < half:
                right_ask(d + 1, 1).start()
                left_ask(d, 0).wait_recv()
                if d + 1 < half:
                    left_ask(d + 1, 1).start()
                load_ids(2 * d).start()
            load_ids(2 * d - 1).start()

        def run():
            if c == 0:
                ask()
            if d < half:
                right(d, c, 0).wait_recv()
                if by_right(d + 1, c):
                    right(d + 1, c, 1).start()
                left(d, c, 0).wait_recv()
                if by_left(d + 1, c):
                    left(d + 1, c, 1).start()
            else:
                right(d, c, 0).wait_recv()
                left(d, c + CHUNKS // 2, 0).wait_recv()

        return run

    for t in range(turns):
        moves[t].append(z_turn(t // CHUNKS + 1, t % CHUNKS))

    def cls_arrives(k):
        def run():
            block = source(k, core)
            g_copy(block, cls_sem.at[k], sibling).wait_recv()
            if k < side:
                for b in range(1, side):
                    g_copy(block, cls_sem.at[b * side + k], target(0, b)).start()
            g_copy(block, sib_sem.at[k], sibling).start()

        return run

    def sib_arrives(k):
        return lambda: g_copy(source(k, 1 - core), sib_sem.at[k], sibling).wait_recv()

    order = [(0, 0)]
    for k in range(1, plane):
        t = 0 if k < side else min(turns - 1, side + 5 * (k - side) // 4)
        moves[t].append(cls_arrives(k))
        order.append((max(t, min(turns - 1, 2 * k - 2)), k))
    for k in range(plane):
        t = min(turns, 2 * k + 1)
        moves[t].append(sib_arrives(k))
        order.append((t, plane + k))
    order.sort()
    first = 0
    while first < ng:
        ns = [n for _, n in order[first : first + 8]]
        last_turn = order[min(ng, first + 8) - 1][0]
        sums[last_turn + 1].append(functools.partial(batch_finish, ns))
        moves[last_turn + 2].append(functools.partial(batch_send, ns))
        first += 8
    for t, n in order:
        sums[t].append(functools.partial(batch_unit, n))

    def ids_arrive(ns):
        for n in ns:
            load_ids(n).wait()

    def mem_start():
        load_mem.wait()
        load_pos.wait()
        ids_arrive([0])

    moves[0].insert(0, mem_start)
    for part in range(3):
        sums[0].append(functools.partial(memory_unit, 0, part))
    sums[1].append(functools.partial(memory_finish, [0]))
    for d in range(1, half + 1):
        ns = [2 * d - 1, 2 * d] if d < half else [2 * d - 1]
        start = CHUNKS * d - 1 if d < half else turns - 1
        moves[start].append(functools.partial(ids_arrive, ns))
        units = [(n, part) for n in ns for part in range(3)]
        spread = CHUNKS if d + 1 < half else 2
        if d == half:
            spread = 1
        for i, (n, part) in enumerate(units):
            sums[start + i * spread // len(units)].append(functools.partial(memory_unit, n, part))
        sums[start + spread].append(functools.partial(memory_finish, ns))
        moves[start + spread + 1].append(functools.partial(memory_send, ns))

    for t in range(turns + 4):
        for move in moves[t]:
            move()
        for work in sums[t]:
            work()

    pltpu.make_async_copy(row_in.at[pl.ds(0, zs - 1)], row_in.at[pl.ds(0, zs - 1)], row_sem).wait()
    got = jnp.concatenate([row_in[o] for o in range(zs)], axis=0)
    spread = lax.dot_general(
        got, onehot, (((0,), (0,)), ((), ())), preferred_element_type=F32, precision=lax.Precision.HIGHEST
    )
    picked = jnp.sum(jnp.where(place, spread, 0.0), axis=0, keepdims=True)
    sub8 = iota((Q, LANES), 0)
    scores = jnp.zeros((Q, LANES), F32)
    count = jnp.zeros((Q, LANES), I32)
    for q in range(Q):
        h, j = q // 4, q % 4
        row = picked[:, h * LANES : (h + 1) * LANES]
        if j:
            row = pltpu.roll(row, LANES - j * LIVE, 1)
        scores = jnp.where(sub8 == q, row, scores)
        count = jnp.where(sub8 == q, cnt_ref[0, q], count)
    valid = lane8 < count
    scores = jnp.where(valid, scores, 0.0)
    out_m[...] = scores[:, : out_m.shape[1]]

    pltpu.make_async_copy(tile_in.at[pl.ds(0, ng - 1)], tile_in.at[pl.ds(0, ng - 1)], tile_sem).wait()
    turned_scores = tile_in[...].reshape(ng * 8, LANES).T
    order = [0, 32, 64, 96, 16, 48, 80, 112]
    rows = jnp.concatenate([turned_scores[o : o + 1] for o in order], axis=0)
    out_b[...] = rows
    top = jnp.maximum(
        jnp.max(rows, axis=1, keepdims=True),
        jnp.max(jnp.where(valid, scores, -jnp.inf), axis=1, keepdims=True),
    )
    total = jnp.sum(jnp.exp(rows - top), axis=1, keepdims=True) + jnp.sum(
        jnp.where(valid, jnp.exp(scores - top), 0.0), axis=1, keepdims=True
    )
    mine = iota(rows.shape, 1) == g * Q + iota(rows.shape, 0)
    own = jnp.sum(jnp.where(mine, rows, 0.0), axis=1, keepdims=True)
    loss = top + jnp.log(total) - own
    spread_loss = jnp.where(lane8 == sub8, loss, 0.0)
    out_l[...] = jnp.sum(spread_loss, axis=0, keepdims=True)[:, :Q]

    items = zs - 1
    pltpu.make_async_copy(zbuf.at[pl.ds(0, items)], zbuf.at[pl.ds(0, items)], zsend_sem).wait()
    pltpu.make_async_copy(gbuf.at[pl.ds(0, ng - 1)], gbuf.at[pl.ds(0, ng - 1)], gsend_sem).wait()
    pltpu.make_async_copy(asks.at[pl.ds(0, items)], asks.at[pl.ds(0, items)], asend_sem).wait()
    pltpu.make_async_copy(row_in.at[pl.ds(0, items)], row_in.at[pl.ds(0, items)], row_send_sem).wait()
    pltpu.make_async_copy(tile_in.at[pl.ds(0, ng - 1)], tile_in.at[pl.ds(0, ng - 1)], tile_send_sem).wait()


def body(queries, positives, memory, candidates, counts):
    zs = lax.axis_size("memory")
    ng = lax.axis_size("group")
    side = math.isqrt(ng // 2)
    assert ng == 2 * side * side and zs == side * side
    width = queries.shape[3]
    p_local = memory.shape[1]
    any_space = pl.BlockSpec(memory_space=pltpu.HBM)
    vmem = pl.BlockSpec(memory_space=pltpu.VMEM)
    smem = pl.BlockSpec(memory_space=pltpu.SMEM)
    dma = pltpu.SemaphoreType.DMA
    slots = candidates.shape[2]
    out_b, out_m, out_l = pl.pallas_call(
        functools.partial(kernel, zs, side),
        out_shape=(
            jax.ShapeDtypeStruct((Q, ng * Q), F32),
            jax.ShapeDtypeStruct((Q, slots), F32),
            jax.ShapeDtypeStruct((1, Q), F32),
        ),
        in_specs=[any_space, any_space, any_space, vmem, smem],
        out_specs=(vmem, vmem, vmem),
        scratch_shapes=[
            pltpu.VMEM((COLS, width), BF16),
            pltpu.VMEM((Q * LANES, width), BF16),
            pltpu.VMEM((p_local, LANES, width), BF16),
            pltpu.VMEM((zs, width, COLS), BF16),
            pltpu.VMEM((ng, width, COLS), BF16),
            pltpu.VMEM((zs, zs // 2, 1, LANES), I32),
            pltpu.SMEM((zs, 1, LANES), I32),
            pltpu.VMEM((ng, 8, COLS), F32),
            pltpu.VMEM((zs, CAP, COLS), F32),
            pltpu.VMEM((zs, 1, LANES), F32),
            pltpu.VMEM((zs, 1, LANES), F32),
            pltpu.VMEM((ng, 8, LANES), F32),
            pltpu.VMEM((ng, 8, LANES), F32),
            dma((3,)), dma((zs // 2 * CHUNKS,)), dma((zs // 2 * CHUNKS,)), dma((zs // 2,)), dma((zs // 2,)),
            dma((zs,)), dma((ng // 2,)), dma((ng // 2,)), dma, dma,
            dma, dma, dma, dma, dma,
        ],
        compiler_params=pltpu.CompilerParams(
            collective_id=0, has_side_effects=True, vmem_limit_bytes=56 * 1024 * 1024
        ),
        cost_estimate=pl.CostEstimate(flops=5 * 10**9, bytes_accessed=5 * 10**6, transcendentals=4096),
        name="scores",
    )(
        queries[0].reshape(COLS, width),
        positives[0].reshape(Q * LANES, width),
        memory[0],
        candidates[0],
        counts,
    )
    return out_b[None], out_m[None], out_l


def solution(mesh):
    in_specs = (
        P("group", "memory", None, None),
        P("group", "memory", None, None),
        P("group", "memory", None, None),
        P("group", "memory", None),
        P("group", "memory"),
    )
    out_specs = (P("group", "memory", None), P("group", "memory", None), P("group", "memory"))
    return jax.shard_map(body, mesh=mesh, in_specs=in_specs, out_specs=out_specs, check_vma=False)
```

time: 76.1 us -> 58.7 us (0.77)
  Pallas kernels: 67.9 us -> 53.5 us
  local copies, waits for them, and re-layouts: 7.01 us -> 3.74 us
    pallas_call x1, Pallas kernels: 67.9 us -> 53.5 us  [body(): pl.pallas_call(functools.partial(kernel, zs, side), out_shape=(jax.ShapeD...]
    unnamed x13 -> x3, local copies, waits for them, and re-layouts: 7.01 us -> 3.74 us
where the time goes in v2:
time: 58.7 us; the launch traced here: 57.9 us
  Pallas kernels  53.5 us (91%)
  local copies, waits for them, and re-layouts  3.74 us (6%)
  between operations  0.64 us (1%)
    pallas_call x1, Pallas kernels, body(): pl.pallas_call(functools.partial(kernel, zs, side), out_shape=(jax.ShapeD...  53.5 us
    unnamed x3, local copies, waits for them, and re-layouts  3.74 us

profile of v2, /device:TPU:1, one launch (start us, length us, event | category | flops | bytes accessed | tf_op | source)
XLA Modules:
  0.0 57.9 jit_solution(7905908460604981227)
XLA Ops:
  0.6 53.5 %scores.1 = (f32[8,256]{1,0:T(8,128)}, f32[8,64]{1,0:T(8,128)}, f32[1,8]{1,0:T(1,128)}) custom-call(bf16[256,128]{1,0:T(8,128)(2,1)} %bitcast.10, bf16[1024,128]{1,0:T(8,128)(2,1)} %bitcast.9, bf16[128,128,128]{2,1,0:T(8,128)(2,1)} %bitcast.8, s32[8,64]{1,0:T(8,128)} %bitcast.11, s32[1,8]{1,0:T(1,128)} %cnt_ref.1), custom_call_target="tpu_custom_call" | custom-call | flops 5000000000 | bytes 5000000 | tf_op jit(solution)/shard_map/scores/pallas_call | solution.py:391
  54.2 1.3 %copy.11 = f32[1,8,256]{2,1,0:T(8,128)} copy(f32[1,8,256]{2,1,0:T(8,128)} %bitcast.6) | data formatting | bytes 16384
  55.5 1.3 %copy.12 = f32[1,8,64]{2,1,0:T(8,128)} copy(f32[1,8,64]{2,1,0:T(8,128)} %bitcast.7) | data formatting | bytes 4096
  56.7 1.2 %copy.13 = f32[1,8]{1,0:T(1,128)} copy(f32[1,8]{1,0:T(1,128)} %get-tuple-element.14) | data formatting | bytes 64

commit v3 on v2

--- a/solution.py
+++ b/solution.py
@@ -18,7 +18,7 @@
 LIVE = 32
 LANES = 128
 COLS = Q * TOK
-CHUNKS = 4
+CHUNKS = 2
 
 
 def iota(shape, axis):
@@ -40,8 +40,6 @@
     core = g & 1
     px = (g >> 1) & (side - 1)
     py = g >> (1 + side_bits)
-    z_right = (z + 1) & (zs - 1)
-    z_left = (z + zs - 1) & (zs - 1)
     sibling = g + 1 - 2 * core
 
     def source(k, c):
@@ -66,12 +64,84 @@
     load_mem.start()
 
     barrier = pltpu.get_barrier_semaphore()
-    partners = [(z_right, g), (z_left, g), (z, sibling)]
+    partners = [((z + o) & (zs - 1), g) for o in (1, -1, 2, -2)] + [(z, sibling)]
     for a in range(1, side):
         partners += [(z, target(a, 0)), (z, target(0, a))]
     for to in partners:
         pl.semaphore_signal(barrier, inc=1, device_id=to, device_id_type=MESH)
 
+    load_q.wait()
+    turned = qv[...].astype(F32).T.astype(BF16)
+    zbuf[z] = turned
+    gbuf[g] = turned
+
+    pl.semaphore_wait(barrier, len(partners))
+
+    def ring_copy(ref, send, recv, to):
+        return pltpu.make_async_remote_copy(
+            src_ref=ref, dst_ref=ref, send_sem=send, recv_sem=recv, device_id=(to, g), device_id_type=MESH
+        )
+
+    def right(d, c, step):
+        block = (z - d + step) & (zs - 1)
+        ref = zbuf.at[block, pl.ds(c * rows_of, rows_of)]
+        return ring_copy(ref, zsend_sem, zr_sem.at[(d - 1) * CHUNKS + c], (z + max(step, 1)) & (zs - 1))
+
+    def left(d, c, step):
+        block = (z + d - step) & (zs - 1)
+        ref = zbuf.at[block, pl.ds(c * rows_of, rows_of)]
+        return ring_copy(ref, zsend_sem, zl_sem.at[(d - 1) * CHUNKS + c], (z - max(step, 1)) & (zs - 1))
+
+    def right_ask(d, step):
+        return ring_copy(asks.at[(z - d + step) & (zs - 1)], asend_sem, ar_sem.at[d - 1], (z + max(step, 1)) & (zs - 1))
+
+    def left_ask(d, step):
+        return ring_copy(asks.at[(z + d - step) & (zs - 1)], asend_sem, al_sem.at[d - 1], (z - max(step, 1)) & (zs - 1))
+
+    def by_right(d, c):
+        return d < half or (d == half and c < CHUNKS // 2)
+
+    def by_left(d, c):
+        return d < half or (d == half and c >= CHUNKS // 2)
+
+    def pass_on(d, c):
+        for step in (2, 1):
+            if by_right(d + step, c):
+                right(d + step, c, step).start()
+            if by_left(d + step, c):
+                left(d + step, c, step).start()
+
+    def pass_asks_right(d):
+        for step in (2, 1):
+            if d + step <= half:
+                right_ask(d + step, step).start()
+
+    def pass_asks_left(d):
+        for step in (2, 1):
+            if d + step < half:
+                left_ask(d + step, step).start()
+
+    def g_copy(block, sem, to):
+        ref = gbuf.at[block]
+        return pltpu.make_async_remote_copy(
+            src_ref=ref, dst_ref=ref, send_sem=gsend_sem, recv_sem=sem,
+            device_id=(z, to), device_id_type=MESH,
+        )
+
+    def asker_of(n):
+        d = (n + 1) // 2
+        return (z - d if n % 2 else z + d) & (zs - 1)
+
+    def load_ids(n):
+        return pltpu.make_async_copy(asks.at[asker_of(n), z >> 1], ids.at[n], id_sem.at[n])
+
+    for c in range(CHUNKS):
+        pass_on(0, c)
+    for a in range(1, side):
+        g_copy(g, cls_sem.at[a], target(a, 0)).start()
+    g_copy(g, sib_sem.at[0], sibling).start()
+    for b in range(1, side):
+        g_copy(g, cls_sem.at[b * side], target(0, b)).start()
     lane = iota((1, LANES), 1)
     cand = jnp.concatenate([cand_ref[...], jnp.zeros((Q, LANES - cand_ref.shape[1]), I32)], axis=1)
     parts, limits = [], []
@@ -106,67 +176,8 @@
     for o in range(zs // 2):
         asks[z, o] = code[2 * o : 2 * o + 1] + pltpu.roll(code[2 * o + 1 : 2 * o + 2], 64, 1)
 
-    load_q.wait()
-    turned = qv[...].astype(F32).T.astype(BF16)
-    zbuf[z] = turned
-    gbuf[g] = turned
-
-    pl.semaphore_wait(barrier, len(partners))
-
-    def ring_copy(ref, send, recv, to):
-        return pltpu.make_async_remote_copy(
-            src_ref=ref, dst_ref=ref, send_sem=send, recv_sem=recv, device_id=(to, g), device_id_type=MESH
-        )
-
-    def right(d, c, step):
-        block = (z - d + step) & (zs - 1)
-        ref = zbuf.at[block, pl.ds(c * rows_of, rows_of)]
-        return ring_copy(ref, zsend_sem, zr_sem.at[(d - 1) * CHUNKS + c], z_right)
-
-    def left(d, c, step):
-        block = (z + d - step) & (zs - 1)
-        ref = zbuf.at[block, pl.ds(c * rows_of, rows_of)]
-        return ring_copy(ref, zsend_sem, zl_sem.at[(d - 1) * CHUNKS + c], z_left)
-
-    def right_ask(d, step):
-        return ring_copy(asks.at[(z - d + step) & (zs - 1)], asend_sem, ar_sem.at[d - 1], z_right)
-
-    def left_ask(d, step):
-        return ring_copy(asks.at[(z + d - step) & (zs - 1)], asend_sem, al_sem.at[d - 1], z_left)
-
-    def by_right(d, c):
-        return d < half or (d == half and c < CHUNKS // 2)
-
-    def by_left(d, c):
-        return d < half or (d == half and c >= CHUNKS // 2)
-
-    def g_copy(block, sem, to):
-        ref = gbuf.at[block]
-        return pltpu.make_async_remote_copy(
-            src_ref=ref, dst_ref=ref, send_sem=gsend_sem, recv_sem=sem,
-            device_id=(z, to), device_id_type=MESH,
-        )
-
-    def asker_of(n):
-        d = (n + 1) // 2
-        return (z - d if n % 2 else z + d) & (zs - 1)
-
-    def load_ids(n):
-        return pltpu.make_async_copy(asks.at[asker_of(n), z >> 1], ids.at[n], id_sem.at[n])
-
-    right_ask(1, 1).start()
-    if half > 1:
-        left_ask(1, 1).start()
-    for c in range(CHUNKS):
-        if by_right(1, c):
-            right(1, c, 1).start()
-        if by_left(1, c):
-            left(1, c, 1).start()
-    for a in range(1, side):
-        g_copy(g, cls_sem.at[a], target(a, 0)).start()
-    g_copy(g, sib_sem.at[0], sibling).start()
-    for b in range(1, side):
-        g_copy(g, cls_sem.at[b * side], target(0, b)).start()
+    pass_asks_right(0)
+    pass_asks_left(0)
     load_ids(0).start()
 
     def best(passages, tokens):
@@ -230,39 +241,38 @@
                     device_id=(asker_of(n), g), device_id_type=MESH,
                 ).start()
 
-    turns = CHUNKS * (half - 1) + CHUNKS // 2
-    moves = [[] for _ in range(turns + 4)]
-    sums = [[] for _ in range(turns + 4)]
+    turns = CHUNKS * half
+    moves = [[] for _ in range(turns + 5)]
+    sums = [[] for _ in range(turns + 5)]
 
     def z_turn(d, c):
-        def ask():
-            right_ask(d, 0).wait_recv()
-            if d < half:
-                right_ask(d + 1, 1).start()
-                left_ask(d, 0).wait_recv()
-                if d + 1 < half:
-                    left_ask(d + 1, 1).start()
-                load_ids(2 * d).start()
-            load_ids(2 * d - 1).start()
-
         def run():
             if c == 0:
-                ask()
-            if d < half:
+                right_ask(d, 0).wait_recv()
+                if d % 2 == 0:
+                    pass_asks_right(d)
+                if d < half:
+                    left_ask(d, 0).wait_recv()
+                    if d % 2 == 0:
+                        pass_asks_left(d)
+                    load_ids(2 * d).start()
+                load_ids(2 * d - 1).start()
+            if by_right(d, c):
                 right(d, c, 0).wait_recv()
-                if by_right(d + 1, c):
-                    right(d + 1, c, 1).start()
+            if by_left(d, c):
                 left(d, c, 0).wait_recv()
-                if by_left(d + 1, c):
-                    left(d + 1, c, 1).start()
-            else:
-                right(d, c, 0).wait_recv()
-                left(d, c + CHUNKS // 2, 0).wait_recv()
+            if d % 2 == 0:
+                pass_on(d, c)
 
         return run
 
-    for t in range(turns):
-        moves[t].append(z_turn(t // CHUNKS + 1, t % CHUNKS))
+    line = []
+    for d in range(2, half, 2):
+        for c in range(CHUNKS):
+            line += [(d, c), (d - 1, c)]
+    line += [(half - 1, c) for c in range(CHUNKS)] + [(half, c) for c in range(CHUNKS)]
+    for t, (d, c) in enumerate(line):
+        moves[t].append(z_turn(d, c))
 
     def cls_arrives(k):
         def run():
@@ -279,12 +289,14 @@
         return lambda: g_copy(source(k, 1 - core), sib_sem.at[k], sibling).wait_recv()
 
     order = [(0, 0)]
+    arrival = [0] * plane
     for k in range(1, plane):
-        t = 0 if k < side else min(turns - 1, side + 5 * (k - side) // 4)
+        t = 2 if k < side else min(turns - 1, 2 * side + 5 * (k - side) // 4)
         moves[t].append(cls_arrives(k))
+        arrival[k] = t
         order.append((max(t, min(turns - 1, 2 * k - 2)), k))
     for k in range(plane):
-        t = min(turns, 2 * k + 1)
+        t = min(turns, max(2 * k + 1, arrival[k] + 2))
         moves[t].append(sib_arrives(k))
         order.append((t, plane + k))
     order.sort()
@@ -313,22 +325,32 @@
     sums[1].append(functools.partial(memory_finish, [0]))
     for d in range(1, half + 1):
         ns = [2 * d - 1, 2 * d] if d < half else [2 * d - 1]
-        start = CHUNKS * d - 1 if d < half else turns - 1
+        start = line.index((d, CHUNKS - 1))
         moves[start].append(functools.partial(ids_arrive, ns))
         units = [(n, part) for n in ns for part in range(3)]
-        spread = CHUNKS if d + 1 < half else 2
-        if d == half:
-            spread = 1
+        spread = 1 if d == half else CHUNKS - 1
+        if d % 2 and d + 1 < half:
+            start += spread
         for i, (n, part) in enumerate(units):
             sums[start + i * spread // len(units)].append(functools.partial(memory_unit, n, part))
         sums[start + spread].append(functools.partial(memory_finish, ns))
         moves[start + spread + 1].append(functools.partial(memory_send, ns))
 
-    for t in range(turns + 4):
+    for t in range(turns + 5):
         for move in moves[t]:
             move()
         for work in sums[t]:
             work()
+
+    pltpu.make_async_copy(tile_in.at[pl.ds(0, ng - 1)], tile_in.at[pl.ds(0, ng - 1)], tile_sem).wait()
+    turned_scores = tile_in[...].reshape(ng * 8, LANES).T
+    order = [0, 32, 64, 96, 16, 48, 80, 112]
+    rows = jnp.concatenate([turned_scores[o : o + 1] for o in order], axis=0)
+    out_b[...] = rows
+    most = jnp.max(rows, axis=1, keepdims=True)
+    mine = iota(rows.shape, 1) == g * Q + iota(rows.shape, 0)
+    own = jnp.sum(jnp.where(mine, rows, 0.0), axis=1, keepdims=True)
+    gathered = jnp.sum(jnp.exp(rows - most), axis=1, keepdims=True)
 
     pltpu.make_async_copy(row_in.at[pl.ds(0, zs - 1)], row_in.at[pl.ds(0, zs - 1)], row_sem).wait()
     got = jnp.concatenate([row_in[o] for o in range(zs)], axis=0)
@@ -350,20 +372,10 @@
     scores = jnp.where(valid, scores, 0.0)
     out_m[...] = scores[:, : out_m.shape[1]]
 
-    pltpu.make_async_copy(tile_in.at[pl.ds(0, ng - 1)], tile_in.at[pl.ds(0, ng - 1)], tile_sem).wait()
-    turned_scores = tile_in[...].reshape(ng * 8, LANES).T
-    order = [0, 32, 64, 96, 16, 48, 80, 112]
-    rows = jnp.concatenate([turned_scores[o : o + 1] for o in order], axis=0)
-    out_b[...] = rows
-    top = jnp.maximum(
-        jnp.max(rows, axis=1, keepdims=True),
-        jnp.max(jnp.where(valid, scores, -jnp.inf), axis=1, keepdims=True),
-    )
-    total = jnp.sum(jnp.exp(rows - top), axis=1, keepdims=True) + jnp.sum(
+    top = jnp.maximum(most, jnp.max(jnp.where(valid, scores, -jnp.inf), axis=1, keepdims=True))
+    total = gathered * jnp.exp(most - top) + jnp.sum(
         jnp.where(valid, jnp.exp(scores - top), 0.0), axis=1, keepdims=True
     )
-    mine = iota(rows.shape, 1) == g * Q + iota(rows.shape, 0)
-    own = jnp.sum(jnp.where(mine, rows, 0.0), axis=1, keepdims=True)
     loss = top + jnp.log(total) - own
     spread_loss = jnp.where(lane8 == sub8, loss, 0.0)
     out_l[...] = jnp.sum(spread_loss, axis=0, keepdims=True)[:, :Q]
@@ -374,6 +386,12 @@
     pltpu.make_async_copy(asks.at[pl.ds(0, items)], asks.at[pl.ds(0, items)], asend_sem).wait()
     pltpu.make_async_copy(row_in.at[pl.ds(0, items)], row_in.at[pl.ds(0, items)], row_send_sem).wait()
     pltpu.make_async_copy(tile_in.at[pl.ds(0, ng - 1)], tile_in.at[pl.ds(0, ng - 1)], tile_send_sem).wait()
+
+
+def hand_over(in_b, in_m, in_l, out_b, out_m, out_l):
+    out_b[...] = in_b[...]
+    out_m[...] = in_m[...]
+    out_l[...] = in_l[...]
 
 
 def body(queries, positives, memory, candidates, counts):
@@ -427,6 +445,13 @@
         candidates[0],
         counts,
     )
+    out_b, out_m, out_l = pl.pallas_call(
+        hand_over,
+        out_shape=tuple(jax.ShapeDtypeStruct(x.shape, F32) for x in (out_b, out_m, out_l)),
+        in_specs=[vmem, vmem, vmem],
+        out_specs=(vmem, vmem, vmem),
+        name="results",
+    )(out_b, out_m, out_l)
     return out_b[None], out_m[None], out_l
 
 

time: 58.7 us -> 51.9 us (0.88)
  local copies, waits for them, and re-layouts: 3.74 us -> 0 us
  Pallas kernels: 53.5 us -> 51.1 us
    pallas_call x1, Pallas kernels: 53.5 us -> 49.7 us  [body(): pl.pallas_call(functools.partial(kernel, zs, side), out_shape=(jax.ShapeD...]
    unnamed x3 -> x0, local copies, waits for them, and re-layouts: 3.74 us -> none
    pallas_call x0 -> x1, Pallas kernels: none -> 1.31 us  [body(): pl.pallas_call(hand_over, out_shape=tuple((jax.ShapeDtypeStruct(x.shape,...]
where the time goes in v3:
time: 51.9 us; the launch traced here: 51.7 us
  Pallas kernels  51.1 us (98%)
  between operations  0.64 us (1%)
    pallas_call x1, Pallas kernels, body(): pl.pallas_call(functools.partial(kernel, zs, side), out_shape=(jax.ShapeD...  49.7 us
    pallas_call x1, Pallas kernels, body(): pl.pallas_call(hand_over, out_shape=tuple((jax.ShapeDtypeStruct(x.shape,...  1.31 us

profile of v3, /device:TPU:1, one launch (start us, length us, event | category | flops | bytes accessed | tf_op | source)
XLA Modules:
  0.0 51.7 jit_solution(16882422993292367821)
XLA Ops:
  0.6 49.7 %scores.1 = (f32[8,256]{1,0:T(8,128)}, f32[8,64]{1,0:T(8,128)}, f32[1,8]{1,0:T(1,128)}) custom-call(bf16[256,128]{1,0:T(8,128)(2,1)} %bitcast.8, bf16[1024,128]{1,0:T(8,128)(2,1)} %bitcast.7, bf16[128,128,128]{2,1,0:T(8,128)(2,1)} %bitcast.6, s32[8,64]{1,0:T(8,128)} %bitcast.10, s32[1,8]{1,0:T(1,128)} %cnt_ref.1), custom_call_target="tpu_custom_call" | custom-call | flops 5000000000 | bytes 5000000 | tf_op jit(solution)/shard_map/scores/pallas_call | solution.py:409
  50.4 1.3 %results.1 = (f32[8,256]{1,0:T(8,128)}, f32[8,64]{1,0:T(8,128)}, f32[1,8]{1,0:T(1,128)}) custom-call(f32[8,256]{1,0:T(8,128)} %get-tuple-element.9.in_b, f32[8,64]{1,0:T(8,128)} %get-tuple-element.10.in_m, f32[1,8]{1,0:T(1,128)} %get-tuple-element.11.in_l), custom_call_target="tpu_custom_call" | custom-call | tf_op jit(solution)/shard_map/results/pallas_call | solution.py:448

commit v4 on v3

--- a/solution.py
+++ b/solution.py
@@ -19,6 +19,7 @@
 LANES = 128
 COLS = Q * TOK
 CHUNKS = 2
+BESIDE = 12
 
 
 def iota(shape, axis):
@@ -241,35 +242,42 @@
                     device_id=(asker_of(n), g), device_id_type=MESH,
                 ).start()
 
+    def first_far(turns):
+        return turns // 4
+
     turns = CHUNKS * half
     moves = [[] for _ in range(turns + 5)]
     sums = [[] for _ in range(turns + 5)]
 
     def z_turn(d, c):
+        def ask():
+            right_ask(d, 0).wait_recv()
+            if d % 2 == 0:
+                pass_asks_right(d)
+            if d < half:
+                left_ask(d, 0).wait_recv()
+                if d % 2 == 0:
+                    pass_asks_left(d)
+                load_ids(2 * d).start()
+            load_ids(2 * d - 1).start()
+
         def run():
-            if c == 0:
-                right_ask(d, 0).wait_recv()
-                if d % 2 == 0:
-                    pass_asks_right(d)
-                if d < half:
-                    left_ask(d, 0).wait_recv()
-                    if d % 2 == 0:
-                        pass_asks_left(d)
-                    load_ids(2 * d).start()
-                load_ids(2 * d - 1).start()
             if by_right(d, c):
                 right(d, c, 0).wait_recv()
             if by_left(d, c):
                 left(d, c, 0).wait_recv()
             if d % 2 == 0:
                 pass_on(d, c)
+            if c == (CHUNKS - 1 if d % 2 == 0 and d < half else 0):
+                ask()
 
         return run
 
     line = []
     for d in range(2, half, 2):
         for c in range(CHUNKS):
-            line += [(d, c), (d - 1, c)]
+            line += [(d, c)]
+        line += [(d - 1, c) for c in range(CHUNKS)]
     line += [(half - 1, c) for c in range(CHUNKS)] + [(half, c) for c in range(CHUNKS)]
     for t, (d, c) in enumerate(line):
         moves[t].append(z_turn(d, c))
@@ -289,26 +297,25 @@
         return lambda: g_copy(source(k, 1 - core), sib_sem.at[k], sibling).wait_recv()
 
     order = [(0, 0)]
-    arrival = [0] * plane
     for k in range(1, plane):
-        t = 2 if k < side else min(turns - 1, 2 * side + 5 * (k - side) // 4)
+        t = min(2, turns - 1) if k < side else min(turns - 1, first_far(turns) + (turns - first_far(turns)) * (k - side) // plane)
         moves[t].append(cls_arrives(k))
-        arrival[k] = t
-        order.append((max(t, min(turns - 1, 2 * k - 2)), k))
-    for k in range(plane):
-        t = min(turns, max(2 * k + 1, arrival[k] + 2))
-        moves[t].append(sib_arrives(k))
-        order.append((t, plane + k))
+        arrives = [t, min(turns - 1, t + turns // 8)]
+        moves[arrives[1]].append(sib_arrives(k))
+        for t, n in zip(arrives, (k, plane + k)):
+            order.append((t if k < side + BESIDE else turns + 1, n))
+    moves[1].append(sib_arrives(0))
+    order.append((1, plane))
     order.sort()
-    first = 0
-    while first < ng:
-        ns = [n for _, n in order[first : first + 8]]
-        last_turn = order[min(ng, first + 8) - 1][0]
-        sums[last_turn + 1].append(functools.partial(batch_finish, ns))
-        moves[last_turn + 2].append(functools.partial(batch_send, ns))
-        first += 8
-    for t, n in order:
+    early = [(t, n) for t, n in order if t < turns]
+    late = [n for t, n in order if t >= turns]
+    for t, n in early:
         sums[t].append(functools.partial(batch_unit, n))
+    for first in range(0, len(early), 8):
+        ns = [n for _, n in early[first : first + 8]]
+        t = early[first : first + 8][-1][0]
+        sums[t + 1].append(functools.partial(batch_finish, ns))
+        moves[t + 2].append(functools.partial(batch_send, ns))
 
     def ids_arrive(ns):
         for n in ns:
@@ -326,11 +333,11 @@
     for d in range(1, half + 1):
         ns = [2 * d - 1, 2 * d] if d < half else [2 * d - 1]
         start = line.index((d, CHUNKS - 1))
+        if d % 2 == 0 and d < half:
+            start += 1
         moves[start].append(functools.partial(ids_arrive, ns))
         units = [(n, part) for n in ns for part in range(3)]
-        spread = 1 if d == half else CHUNKS - 1
-        if d % 2 and d + 1 < half:
-            start += spread
+        spread = 1
         for i, (n, part) in enumerate(units):
             sums[start + i * spread // len(units)].append(functools.partial(memory_unit, n, part))
         sums[start + spread].append(functools.partial(memory_finish, ns))
@@ -341,6 +348,13 @@
             move()
         for work in sums[t]:
             work()
+
+    for first in range(0, len(late), 8):
+        ns = late[first : first + 8]
+        for n in ns:
+            batch_unit(n)
+        batch_finish(ns)
+        batch_send(ns)
 
     pltpu.make_async_copy(tile_in.at[pl.ds(0, ng - 1)], tile_in.at[pl.ds(0, ng - 1)], tile_sem).wait()
     turned_scores = tile_in[...].reshape(ng * 8, LANES).T

time: 51.9 us -> 51.1 us (0.985)
  Pallas kernels: 51.1 us -> 50.3 us
    pallas_call x1, Pallas kernels: 49.7 us -> 49 us  [body(): pl.pallas_call(functools.partial(kernel, zs, side), out_shape=(jax.ShapeD...]
where the time goes in v4:
time: 51.1 us; the launch traced here: 50.9 us
  Pallas kernels  50.3 us (98%)
  between operations  0.64 us (1%)
    pallas_call x1, Pallas kernels, body(): pl.pallas_call(functools.partial(kernel, zs, side), out_shape=(jax.ShapeD...  49 us
    pallas_call x1, Pallas kernels, body(): pl.pallas_call(hand_over, out_shape=tuple((jax.ShapeDtypeStruct(x.shape,...  1.31 us

profile of v4, /device:TPU:1, one launch (start us, length us, event | category | flops | bytes accessed | tf_op | source)
XLA Modules:
  0.0 50.9 jit_solution(7429439254236658648)
XLA Ops:
  0.6 49.0 %scores.1 = (f32[8,256]{1,0:T(8,128)}, f32[8,64]{1,0:T(8,128)}, f32[1,8]{1,0:T(1,128)}) custom-call(bf16[256,128]{1,0:T(8,128)(2,1)} %bitcast.8, bf16[1024,128]{1,0:T(8,128)(2,1)} %bitcast.7, bf16[128,128,128]{2,1,0:T(8,128)(2,1)} %bitcast.6, s32[8,64]{1,0:T(8,128)} %bitcast.10, s32[1,8]{1,0:T(1,128)} %cnt_ref.1), custom_call_target="tpu_custom_call" | custom-call | flops 5000000000 | bytes 5000000 | tf_op jit(solution)/shard_map/scores/pallas_call | solution.py:423
  49.6 1.3 %results.1 = (f32[8,256]{1,0:T(8,128)}, f32[8,64]{1,0:T(8,128)}, f32[1,8]{1,0:T(1,128)}) custom-call(f32[8,256]{1,0:T(8,128)} %get-tuple-element.9.in_b, f32[8,64]{1,0:T(8,128)} %get-tuple-element.10.in_m, f32[1,8]{1,0:T(1,128)} %get-tuple-element.11.in_l), custom_call_target="tpu_custom_call" | custom-call | tf_op jit(solution)/shard_map/results/pallas_call | solution.py:462
